TPU v7x, 32 devices: a whole 2x2x4 slice. The times are simulated.
32 devices in a mesh: groups: 2 (over x), tok: 4 (over y, core), hid: 4 (over z).
Axes of the slice: x: 2, y: 2, z: 4, core: 2. Of those that a mesh axis runs over, the one named last changes fastest.
Arguments:
- tokens: bfloat16 [2048, 5376], P(('groups', 'tok'), 'hid'), parts along dimension 0, may hold values from -6 to 6
- w_query: bfloat16 [5376, 2048], P('tok', 'hid'), may hold values from -0.078125 to 0.078125
- key_weight: bfloat16 [5376, 1024], P('tok', 'hid'), may hold values from -0.078125 to 0.078125
- value_weight: bfloat16 [5376, 1024], P('tok', 'hid'), may hold values from -0.078125 to 0.078125
- w_out: bfloat16 [2048, 5376], P('tok', 'hid'), may hold values from -0.5 to 0.5
- query_norm_gain: float32 [128], replicated, may hold values from 0.5 to 2
- key_gain: float32 [128], replicated, may hold values from 0.5 to 2
- positions: int32 [2048], P('groups'), parts along dimension 0, may hold values from 0 to 131071, as said below
- grad_out: bfloat16 [2048, 5376], P(('groups', 'tok'), 'hid'), parts along dimension 0, may hold values from -6 to 6
Outputs:
- attn_out: bfloat16 [2048, 5376], P(('groups', 'tok'), 'hid'), parts along dimension 0
- grad_x: bfloat16 [2048, 5376], P(('groups', 'tok'), 'hid'), parts along dimension 0
- grad_wq: float32 [10752, 2048], P(('groups', 'tok'), 'hid'), parts along dimension 0
- key_weight_gradient: float32 [10752, 1024], P(('groups', 'tok'), 'hid'), parts along dimension 0
- value_weight_gradient: float32 [10752, 1024], P(('groups', 'tok'), 'hid'), parts along dimension 0
- grad_wo: float32 [4096, 5376], P(('groups', 'tok'), 'hid'), parts along dimension 0
There are 2 independent parts, one for each index of `groups`. A program takes and returns all parts, laid end to end along the dimension named above; an argument that names none is the same for every part. Nothing has to cross between parts.
Inputs may be any that keep to these rules, and one draw needn't show every extreme that they name: positions[t] is token t's position in its document: it rises by one from token to token and is 0 where a document begins; the first document begins before the window and its last token in the window has position 131071; at least one document begins inside the window.
All inputs are finite; a program needn't handle non-finite values.
Results may differ from a plain program's by a relative error of at most 0.02.
Values may be sent and summed in bfloat16 or wider, within the bound.
A program may use at most 192 MiB of HBM per device.

v0:
```python
import jax
import jax.numpy as jnp
from jax import lax
from jax.sharding import PartitionSpec as P

QUERY_HEADS = 16
KEY_VALUE_HEADS = 8
HEAD_SIZE = 128
WINDOW = 1024
TOK_DEV = 256
attn_scale = 168.0 ** (-0.5)
rope_base = 10000.0
norm_eps = 1e-06


def from_behind(value, axis, steps):
    count = lax.axis_size(axis)
    first, last = (max(0, -steps), min(count, count - steps))
    return lax.ppermute(value, axis, [(source, source + steps) for source in range(first, last)])


def rotary_tables(token_pos):
    half_dim = HEAD_SIZE // 2
    freqs = rope_base ** (-jnp.arange(half_dim, dtype=jnp.float32) * 2.0 / HEAD_SIZE)
    angles = token_pos.astype(jnp.float32)[:, None] * freqs[None, :]
    return (jnp.cos(angles), jnp.sin(angles))


def prepare_inputs(raw_values, gain_vector, cosine_table, sine_table):
    scaled = (
        raw_values
        * lax.rsqrt(jnp.mean(raw_values * raw_values, -1, keepdims=True) + norm_eps)
        * gain_vector
    )
    half_dim = scaled.shape[-1] // 2
    first_half = scaled[..., :half_dim]
    second_half = scaled[..., half_dim:]
    cos_rows = cosine_table[:, None, :]
    sin_rows = sine_table[:, None, :]
    return jnp.concatenate(
        [
            first_half * cos_rows - second_half * sin_rows,
            second_half * cos_rows + first_half * sin_rows,
        ],
        -1,
    )


def local(
    tokens, w_query, key_weight, value_weight, w_out, query_norm_gain, key_gain, positions, grad_out
):
    hidden_count = lax.axis_size("hid")
    block_index = lax.axis_index("tok")
    query_heads = QUERY_HEADS // hidden_count
    key_value_heads = KEY_VALUE_HEADS // hidden_count
    group_width = QUERY_HEADS // KEY_VALUE_HEADS
    reach = WINDOW // TOK_DEV
    span_rows = (reach + 1) * TOK_DEV
    leading_part = reach * TOK_DEV
    first_token = block_index * TOK_DEV
    query_cols = query_heads * HEAD_SIZE
    kv_cols = key_value_heads * HEAD_SIZE
    full_rows = lax.all_gather(tokens, "hid", axis=1, tiled=True)
    pieces = (
        lax.all_gather(w_query, "tok", axis=0, tiled=True),
        lax.all_gather(key_weight, "tok", axis=0, tiled=True),
        lax.all_gather(value_weight, "tok", axis=0, tiled=True),
    )
    columns = full_rows
    query_unnormed = jnp.dot(columns, pieces[0], preferred_element_type=jnp.float32)
    key_unnormed = jnp.dot(columns, pieces[1], preferred_element_type=jnp.float32)
    value_raw = jnp.dot(columns, pieces[2], preferred_element_type=jnp.float32)
    values_local = value_raw.astype(jnp.bfloat16)
    token_pos = lax.dynamic_slice_in_dim(positions, first_token, TOK_DEV, 0)
    cosine_table, sine_table = rotary_tables(token_pos)
    query_heads_raw = query_unnormed.reshape(TOK_DEV, query_heads, HEAD_SIZE)
    key_heads_raw = key_unnormed.reshape(TOK_DEV, key_value_heads, HEAD_SIZE)
    query_rows = (
        prepare_inputs(query_heads_raw, query_norm_gain, cosine_table, sine_table)
        .astype(jnp.bfloat16)
        .reshape(TOK_DEV, key_value_heads, group_width, HEAD_SIZE)
    )
    keys_local = prepare_inputs(key_heads_raw, key_gain, cosine_table, sine_table).astype(
        jnp.bfloat16
    )
    key_value = jnp.stack([keys_local.reshape(TOK_DEV, kv_cols), values_local], 0)
    blocks = [key_value]
    moving = key_value
    for turn_index in range(reach):
        moving = from_behind(moving, "tok", 1)
        blocks = [moving] + blocks
    window = jnp.concatenate(blocks, 1)
    key_window = window[0].reshape(span_rows, key_value_heads, HEAD_SIZE)
    value_window = window[1].reshape(span_rows, key_value_heads, HEAD_SIZE)
    query_index = first_token + jnp.arange(TOK_DEV, dtype=jnp.int32)
    key_index = first_token - leading_part + jnp.arange(span_rows, dtype=jnp.int32)
    padded_pos = jnp.pad(positions, (leading_part, 0))
    key_pos = lax.dynamic_slice_in_dim(padded_pos, first_token, span_rows, 0)
    distance = query_index[:, None] - key_index[None, :]
    allowed = (
        (key_index[None, :] >= 0)
        & (distance >= 0)
        & (distance < WINDOW)
        & (token_pos[:, None] - key_pos[None, :] == distance)
    )
    scores = (
        jnp.einsum("tkgd,ukd->kgtu", query_rows, key_window, preferred_element_type=jnp.float32)
        * attn_scale
    )
    weights = jnp.where(allowed[None, None], jnp.exp(scores), 0.0)
    probabilities = weights / jnp.sum(weights, -1, keepdims=True)
    rounded = probabilities.astype(jnp.bfloat16)
    attended = jnp.einsum(
        "kgtu,ukd->tkgd", rounded, value_window, preferred_element_type=jnp.float32
    )
    attended = attended.astype(jnp.bfloat16).reshape(TOK_DEV, query_cols)
    all_heads = lax.all_gather(attended, "hid", axis=1, tiled=True)
    columns = all_heads
    output = jnp.dot(
        columns,
        lax.all_gather(w_out, "tok", axis=0, tiled=True),
        preferred_element_type=jnp.float32,
    )
    attn_out = output.astype(jnp.bfloat16)
    partial_heads = jnp.einsum(
        "td,hd->th",
        grad_out,
        lax.all_gather(w_out, "tok", axis=0, tiled=True),
        preferred_element_type=jnp.float32,
    )
    attended_gradient = lax.psum_scatter(
        partial_heads.astype(jnp.bfloat16), "hid", scatter_dimension=1, tiled=True
    )
    attended_gradient = attended_gradient.reshape(TOK_DEV, key_value_heads, group_width, HEAD_SIZE)
    columns = all_heads
    grad_wo = lax.psum_scatter(
        jnp.einsum("th,td->hd", columns, grad_out, preferred_element_type=jnp.float32).astype(
            jnp.bfloat16
        ),
        "tok",
        scatter_dimension=0,
        tiled=True,
    ).astype(jnp.float32)
    grad_probs = jnp.einsum(
        "tkgd,ukd->kgtu", attended_gradient, value_window, preferred_element_type=jnp.float32
    )
    grad_scores = (
        attn_scale
        * probabilities
        * (grad_probs - jnp.sum(probabilities * grad_probs, -1, keepdims=True))
    )
    grad_scores = grad_scores.astype(jnp.bfloat16)
    grad_queries = jnp.einsum(
        "kgtu,ukd->tkgd", grad_scores, key_window, preferred_element_type=jnp.float32
    )
    keys_gradient = jnp.einsum(
        "kgtu,tkgd->ukd", grad_scores, query_rows, preferred_element_type=jnp.float32
    )
    values_gradient = jnp.einsum(
        "kgtu,tkgd->ukd", rounded, attended_gradient, preferred_element_type=jnp.float32
    )
    grad_window = jnp.stack(
        [keys_gradient.reshape(span_rows, kv_cols), values_gradient.reshape(span_rows, kv_cols)], 0
    )
    grad_kv = grad_window[:, :TOK_DEV]
    for turn_index in range(1, reach + 1):
        grad_kv = (
            from_behind(grad_kv.astype(jnp.bfloat16), "tok", -1).astype(grad_kv.dtype)
            + grad_window[:, turn_index * TOK_DEV : (turn_index + 1) * TOK_DEV]
        )
    _, query_pull = jax.vjp(
        lambda raw_values: prepare_inputs(raw_values, query_norm_gain, cosine_table, sine_table),
        query_heads_raw,
    )
    _, key_pullback = jax.vjp(
        lambda raw_values: prepare_inputs(raw_values, key_gain, cosine_table, sine_table),
        key_heads_raw,
    )
    query_back = (
        query_pull(grad_queries.reshape(TOK_DEV, query_heads, HEAD_SIZE))[0]
        .astype(jnp.bfloat16)
        .reshape(TOK_DEV, query_cols)
    )
    key_backward = (
        key_pullback(grad_kv[0].reshape(TOK_DEV, key_value_heads, HEAD_SIZE))[0]
        .astype(jnp.bfloat16)
        .reshape(TOK_DEV, kv_cols)
    )
    value_backward = grad_kv[1].astype(jnp.bfloat16)
    pieces = (
        lax.all_gather(w_query, "tok", axis=0, tiled=True),
        lax.all_gather(key_weight, "tok", axis=0, tiled=True),
        lax.all_gather(value_weight, "tok", axis=0, tiled=True),
    )
    block_rows = jnp.einsum("tc,dc->td", query_back, pieces[0], preferred_element_type=jnp.float32)
    block_rows = block_rows + jnp.einsum(
        "tc,dc->td", key_backward, pieces[1], preferred_element_type=jnp.float32
    )
    block_rows = block_rows + jnp.einsum(
        "tc,dc->td", value_backward, pieces[2], preferred_element_type=jnp.float32
    )
    grad_x = lax.psum_scatter(
        block_rows.astype(jnp.bfloat16), "hid", scatter_dimension=1, tiled=True
    )
    joined = jnp.concatenate([query_back, key_backward, value_backward], 1)
    columns = full_rows
    inputs_gradient = lax.psum_scatter(
        jnp.einsum("td,tc->dc", columns, joined, preferred_element_type=jnp.float32).astype(
            jnp.bfloat16
        ),
        "tok",
        scatter_dimension=0,
        tiled=True,
    ).astype(jnp.float32)
    grad_wq = inputs_gradient[:, :query_cols]
    key_weight_gradient = inputs_gradient[:, query_cols : query_cols + kv_cols]
    value_weight_gradient = inputs_gradient[:, query_cols + kv_cols :]
    return (attn_out, grad_x, grad_wq, key_weight_gradient, value_weight_gradient, grad_wo)


def solution(mesh):
    return jax.shard_map(
        local,
        mesh=mesh,
        in_specs=(
            P(("groups", "tok"), "hid"),
            P("tok", "hid"),
            P("tok", "hid"),
            P("tok", "hid"),
            P("tok", "hid"),
            P(),
            P(),
            P("groups"),
            P(("groups", "tok"), "hid"),
        ),
        out_specs=(
            P(("groups", "tok"), "hid"),
            P(("groups", "tok"), "hid"),
            P(("groups", "tok"), "hid"),
            P(("groups", "tok"), "hid"),
            P(("groups", "tok"), "hid"),
            P(("groups", "tok"), "hid"),
        ),
        check_vma=False,
    )
```

profile of v0, /device:TPU:0, one launch (start us, length us, event | category | flops | bytes accessed | tf_op | source)
XLA Modules:
  0.0 533.1 jit_solution(8596791121754949615)
XLA Ops:
  12.1 57.2 %all-gather.7.cloned.1.call-done = bf16[256,5376]{0,1:T(8,128)(2,1)} async-done(((bf16[256,1344]{0,1:T(8,128)(2,1)}), bf16[256,5376]{0,1:T(8,128)(2,1)}) %all-gather.7.cloned.1.call-update) | async-done | bytes 2752528 | tf_op jit(solution)/shard_map/all_gather | solution.py:63
  69.3 26.6 %all-gather.9.cloned.1.call-done = bf16[5376,256]{1,0:T(8,128)(2,1)} async-done(((bf16[1344,256]{1,0:T(8,128)(2,1)}), bf16[5376,256]{1,0:T(8,128)(2,1)}) %all-gather.9.cloned.1.call-update) | async-done | bytes 2752528 | tf_op jit(solution)/shard_map/all_gather | solution.py:66
  95.9 3.8 multiply_reduce_fusion.3
  103.0 20.9 %all-gather.11.cloned.1.call-done = bf16[5376,256]{1,0:T(8,128)(2,1)} async-done(((bf16[1344,256]{1,0:T(8,128)(2,1)}), bf16[5376,256]{1,0:T(8,128)(2,1)}) %all-gather.11.cloned.1.call-update) | async-done | bytes 2752528 | tf_op jit(solution)/shard_map/all_gather | solution.py:67
  123.9 2.7 fusion.17
  127.3 2.1 collective-permute-start
  131.3 4.9 collective-permute-start.1
  137.0 12.5 %collective-permute-start.2 = (bf16[2,256,256]{2,1,0:T(8,128)(2,1)}, bf16[2,256,256]{2,1,0:T(8,128)(2,1)}, u32[]{:S(2)}, u32[]{:S(2)}) collective-permute-start(bf16[2,256,256]{2,1,0:T(8,128)(2,1)} %collective-permute-done.1), channel_id=1, source_target_pairs={{0,4},{4,8},{8,12},{1,5},{5,9},{9,13},{2,6},{6,10},{10,14},{3,7},{... | collective-permute-start | bytes 786440 | tf_op jit(solution)/shard_map/ppermute | solution.py:19
  150.3 12.2 %collective-permute-start.3 = (bf16[2,256,256]{2,1,0:T(8,128)(2,1)}, bf16[2,256,256]{2,1,0:T(8,128)(2,1)S(1)}, u32[]{:S(2)}, u32[]{:S(2)}) collective-permute-start(bf16[2,256,256]{2,1,0:T(8,128)(2,1)} %collective-permute-done.2), channel_id=1, source_target_pairs={{0,4},{4,8},{8,12},{1,5},{5,9},{9,13},{2,6},{6,10},{10,14},{3,7},{... | collective-permute-start | bytes 786440 | tf_op jit(solution)/shard_map/ppermute | solution.py:19
  162.5 2.1 fusion.11
  165.3 1.7 constant_dynamic-update-slice_fusion.3
  167.0 1.7 constant_dynamic-update-slice_fusion.2
  170.9 5.3 %convolution_convert_fusion.3 = bf16[256,2048]{1,0:T(8,128)(2,1)} fusion(bf16[256,1344]{0,1:T(8,128)(2,1)S(1)} %copy-done, bf16[2048,1344]{0,1:T(8,128)(2,1)} %all-gather.17.cloned.1.call-done), kind=kOutput, calls=%fused_computation.23 | convolution fusion | flops 1409810432 | bytes 7241728 | tf_op jit(solution)/shard_map/td,hd->th/dot_general | solution.py:125
  176.5 1.7 constant_dynamic-update-slice_fusion
  178.2 2.4 fusion.50
  180.6 2.5 reshape_squeeze.9
  183.2 2.6 reshape_squeeze.10
  185.7 3.0 copy.117
  188.7 29.4 %all-gather.13.cloned.1.call-done = bf16[5376,512]{1,0:T(8,128)(2,1)} async-done(((bf16[1344,512]{1,0:T(8,128)(2,1)}), bf16[5376,512]{1,0:T(8,128)(2,1)}) %all-gather.13.cloned.1.call-update) | async-done | bytes 5505040 | tf_op jit(solution)/shard_map/all_gather | solution.py:65
  218.1 5.0 fusion.53
  225.9 22.1 %reduce-scatter.7.cloned.1.call-done = bf16[256,512]{1,0:T(8,128)(2,1)} async-done(((bf16[256,2048]{1,0:T(8,128)(2,1)}), bf16[256,512]{1,0:T(8,128)(2,1)}) %reduce-scatter.7.cloned.1.call-update) | async-done | bytes 262160 | tf_op jit(solution)/shard_map/reduce_scatter | solution.py:131
  249.1 3.2 fusion.19
  252.3 7.2 %fusion.2 = (f32[2,2,256]{2,1,0:T(2,128)S(1)}, f32[2,2,256,1280]{2,3,1,0:T(8,128)}) fusion(f32[2,1280,256,2]{2,1,3,0:T(8,128)} %fusion.19, bf16[1280,2,128,1]{0,2,3,1:T(8,128)(2,1)S(1)} %copy-done.14, pred[256,1280]{0,1:T(8,128)(4,1)S(1)} %copy-done.34, bf16[256,2,2,64]{3,0,2,1:T(8,128)(2,1)S(1)} %bitcast.103, bf16[256,2,2,64]{3,0,2,1:T(8,128)(2,1)S(1)} %bitcast.105), kind=kOutput, calls=%fused_computation.8 | convolution fusion | flops 342623488 | bytes 11735040 | tf_op jit(solution)/shard_map/div | solution.py:111
  259.5 3.8 fusion.14
  263.3 26.7 %all-gather.15.cloned.1.call-done = bf16[256,2048]{0,1:T(8,128)(2,1)} async-done(((bf16[256,512]{0,1:T(8,128)(2,1)}), bf16[256,2048]{0,1:T(8,128)(2,1)}) %all-gather.15.cloned.1.call-update) | async-done | bytes 1048592 | tf_op jit(solution)/shard_map/all_gather | solution.py:117
  290.0 5.2 convolution_convert_fusion.1
  295.5 4.8 fusion.4
  301.4 4.5 fusion.7
  307.5 2.1 collective-permute-done.4
  314.2 3.2 collective-permute-done.5
  317.4 1.7 fusion.32
  322.5 10.5 %collective-permute-done.6 = bf16[2,256,256]{1,2,0:T(8,128)(2,1)} collective-permute-done((bf16[2,256,256]{1,2,0:T(8,128)(2,1)}, bf16[2,256,256]{1,2,0:T(8,128)(2,1)}, u32[]{:S(2)}, u32[]{:S(2)}) %collective-permute-start.6) | collective-permute-done | bytes 262176 | tf_op jit(solution)/shard_map/ppermute | solution.py:19
  333.0 1.7 fusion.24
  336.2 2.0 fusion.21
  339.0 9.6 %collective-permute-done.7 = bf16[2,256,256]{1,2,0:T(8,128)(2,1)} collective-permute-done((bf16[2,256,256]{1,2,0:T(8,128)(2,1)}, bf16[2,256,256]{1,2,0:T(8,128)(2,1)}, u32[]{:S(2)}, u32[]{:S(2)}) %collective-permute-start.7) | collective-permute-done | bytes 262176 | tf_op jit(solution)/shard_map/ppermute | solution.py:19
  352.2 7.7 %fusion = bf16[5376,1024]{0,1:T(8,128)(2,1)} fusion(bf16[256,5376]{0,1:T(8,128)(2,1)} %all-gather.7.cloned.1.call-done, bf16[256,256]{1,0:T(8,128)(2,1)S(1)} %copy.109, bf16[256,256]{1,0:T(8,128)(2,1)S(1)} %copy.108, bf16[256,512]{1,0:T(8,128)(2,1)S(1)} %bitcast.102), kind=kOutput, calls=%fused_computation.1 | convolution fusion | flops 2825650176 | bytes 14286848 | tf_op jit(solution)/shard_map/td,tc->dc/dot_general | solution.py:208
  359.9 14.7 %copy.133 = bf16[5376,1024]{1,0:T(8,128)(2,1)} copy(bf16[5376,1024]{0,1:T(8,128)(2,1)} %fusion) | data formatting | bytes 22020096
  375.5 4.3 fusion.47
  381.7 2.5 fusion.1
  385.5 5.5 %convolution_convert_fusion.2 = bf16[256,1344]{0,1:T(8,128)(2,1)} fusion(bf16[2048,1344]{0,1:T(8,128)(2,1)} %all-gather.17.cloned.1.call-done, bf16[256,2048]{0,1:T(8,128)(2,1)S(1)} %copy-done.26), kind=kOutput, calls=%fused_computation.22 | convolution fusion | flops 1409630208 | bytes 7241728 | tf_op jit(solution)/shard_map/dot_general | solution.py:119
  391.0 3.6 convert_element_type.111
  394.6 74.7 %reduce-scatter.13.cloned.1.call-done = bf16[1344,1024]{1,0:T(8,128)(2,1)} async-done(((bf16[5376,1024]{1,0:T(8,128)(2,1)}), bf16[1344,1024]{1,0:T(8,128)(2,1)}) %reduce-scatter.13.cloned.1.call-update) | async-done | bytes 2752528
  469.3 4.6 copy.134
  473.9 3.1 slice.82
  477.0 3.8 copy.110
  480.8 2.6 fusion.49
  483.4 2.9 copy.111
  487.8 38.4 %reduce-scatter.9.cloned.1.call-done = bf16[256,1344]{0,1:T(8,128)(2,1)} async-done(((bf16[256,5376]{0,1:T(8,128)(2,1)}), bf16[256,1344]{0,1:T(8,128)(2,1)}) %reduce-scatter.9.cloned.1.call-update) | async-done | bytes 688144 | tf_op jit(solution)/shard_map/reduce_scatter | solution.py:202
  (157 shorter events, 41.0 us)
Async XLA Ops:
  7.2 163.8 %copy-start = (bf16[256,1344]{0,1:T(8,128)(2,1)S(1)}, bf16[256,1344]{0,1:T(8,128)(2,1)}, u32[]{:S(2)}) copy-start(bf16[256,1344]{0,1:T(8,128)(2,1)} %param.17) | copy-start | bytes 2064388
  7.2 3.5 copy-start.36
  7.2 62.1 %all-gather.7.cloned.1.call-start = ((), (), s32[]{:S(2)}) async-start(), calls=%async_computation.4 | async-start | bytes 3440640 | tf_op jit(solution)/shard_map/all_gather | solution.py:63
  7.9 88.0 %all-gather.9.cloned.1.call-start = ((), (), s32[]{:S(2)}) async-start(), calls=%async_computation.5 | async-start | bytes 3440640 | tf_op jit(solution)/shard_map/all_gather | solution.py:66
  8.7 115.2 %all-gather.11.cloned.1.call-start = ((), (), s32[]{:S(2)}) async-start(), calls=%async_computation.6 | async-start | bytes 3440640 | tf_op jit(solution)/shard_map/all_gather | solution.py:67
  9.4 161.5 %all-gather.17.cloned.1.call-start = ((), (), s32[]{:S(2)}) async-start(), calls=%async_computation.9 | async-start | bytes 6881280 | tf_op jit(solution)/shard_map/all_gather | solution.py:121
  10.0 208.1 %all-gather.13.cloned.1.call-start = ((), (), s32[]{:S(2)}) async-start(), calls=%async_computation.7 | async-start | bytes 6881280 | tf_op jit(solution)/shard_map/all_gather | solution.py:65
  10.6 237.4 %reduce-scatter.7.cloned.1.call-start = ((), (), s32[]{:S(2)}) async-start(), calls=%async_computation.10 | async-start | bytes 1310720 | tf_op jit(solution)/shard_map/reduce_scatter | solution.py:131
  12.1 88.4 %copy-start.38 = (f32[128]{0:T(128)S(1)}, f32[128]{0:T(128)}, u32[]{:S(2)}) copy-start(f32[128]{0:T(128)} %param.15) | copy-start | bytes 1540
  69.3 54.6 %copy-start.2 = (bf16[256,5376]{0,1:T(8,128)(2,1)S(1)}, bf16[256,5376]{0,1:T(8,128)(2,1)}, u32[]{:S(2)}) copy-start(bf16[256,5376]{0,1:T(8,128)(2,1)} %all-gather.7.cloned.1.call-done) | copy-start | bytes 8257540
  95.9 4.6 copy-start.31
  123.9 2.8 copy-start.29
  127.3 3.3 collective-permute-start
  131.3 5.8 %collective-permute-start.1 = (bf16[2,256,256]{2,1,0:T(8,128)(2,1)S(1)}, bf16[2,256,256]{2,1,0:T(8,128)(2,1)}, u32[]{:S(2)}, u32[]{:S(2)}) collective-permute-start(bf16[2,256,256]{2,1,0:T(8,128)(2,1)S(1)} %collective-permute-done), channel_id=1, source_target_pairs={{0,4},{4,8},{8,12},{1,5},{5,9},{9,13},{2,6},{6,10},{10,14},{3,7},{... | collective-permute-start | bytes 786440 | tf_op jit(solution)/shard_map/ppermute | solution.py:19
  137.0 13.2 %collective-permute-start.2 = (bf16[2,256,256]{2,1,0:T(8,128)(2,1)}, bf16[2,256,256]{2,1,0:T(8,128)(2,1)}, u32[]{:S(2)}, u32[]{:S(2)}) collective-permute-start(bf16[2,256,256]{2,1,0:T(8,128)(2,1)} %collective-permute-done.1), channel_id=1, source_target_pairs={{0,4},{4,8},{8,12},{1,5},{5,9},{9,13},{2,6},{6,10},{10,14},{3,7},{... | collective-permute-start | bytes 786440 | tf_op jit(solution)/shard_map/ppermute | solution.py:19
  150.3 14.3 %collective-permute-start.3 = (bf16[2,256,256]{2,1,0:T(8,128)(2,1)}, bf16[2,256,256]{2,1,0:T(8,128)(2,1)S(1)}, u32[]{:S(2)}, u32[]{:S(2)}) collective-permute-start(bf16[2,256,256]{2,1,0:T(8,128)(2,1)} %collective-permute-done.2), channel_id=1, source_target_pairs={{0,4},{4,8},{8,12},{1,5},{5,9},{9,13},{2,6},{6,10},{10,14},{3,7},{... | collective-permute-start | bytes 786440 | tf_op jit(solution)/shard_map/ppermute | solution.py:19
  176.3 113.7 %all-gather.15.cloned.1.call-start = ((), (), s32[]{:S(2)}) async-start(), calls=%async_computation.8 | async-start | bytes 1310720 | tf_op jit(solution)/shard_map/all_gather | solution.py:117
  188.7 36.2 %copy-start.37 = (f32[128]{0:T(128)S(1)}, f32[128]{0:T(128)}, u32[]{:S(2)}) copy-start(f32[128]{0:T(128)} %param.14) | copy-start | bytes 1540
  223.0 2.2 copy-start.20
  223.0 2.2 copy-start.22
  224.3 24.8 %copy-start.3 = (f32[256,4,128]{2,1,0:T(4,128)}, f32[256,4,128]{2,1,0:T(4,128)S(1)}, u32[]{:S(2)}) copy-start(f32[256,4,128]{2,1,0:T(4,128)S(1)} %reshape.224) | copy-start | bytes 1572868
  224.3 24.8 %copy-start.6 = (bf16[1280,2,128]{2,1,0:T(2,128)(2,1)S(1)}, bf16[1280,2,128]{2,1,0:T(2,128)(2,1)}, u32[]{:S(2)}) copy-start(bf16[1280,2,128]{2,1,0:T(2,128)(2,1)} %reshape_squeeze.9) | copy-start | bytes 1966084
  224.9 24.2 %copy-start.27 = (f32[256,4]{1,0:T(8,128)}, f32[256,4]{1,0:T(8,128)S(1)}, u32[]{:S(2)}) copy-start(f32[256,4]{1,0:T(8,128)S(1)} %copy.90) | copy-start | bytes 12292
  249.1 3.2 copy-start.17
  249.1 3.2 copy-start.14
  249.1 3.2 copy-start.34
  263.3 127.7 %reduce-scatter.11.cloned.1.call-start = ((), (), s32[]{:S(2)}) async-start(), calls=%async_computation.12 | async-start | bytes 6881280 | tf_op jit(solution)/shard_map/reduce_scatter | solution.py:136
  295.3 174.0 %reduce-scatter.13.cloned.1.call-start = ((), (), s32[]{:S(2)}) async-start(), calls=%async_computation.13 | async-start | bytes 13762560
  306.0 5.7 %copy-start.15 = (bf16[1280,2,128,1]{0,2,3,1:T(8,128)(2,1)S(1)}, bf16[1280,2,128,1]{0,2,3,1:T(8,128)(2,1)}, u32[]{:S(2)}) copy-start(bf16[1280,2,128,1]{0,2,3,1:T(8,128)(2,1)} %copy.117) | copy-start | bytes 1966084
  306.0 3.6 collective-permute-start.4
  310.4 7.1 %collective-permute-start.5 = (bf16[2,256,256]{1,2,0:T(8,128)(2,1)}, bf16[2,256,256]{1,2,0:T(8,128)(2,1)}, u32[]{:S(2)}, u32[]{:S(2)}) collective-permute-start(bf16[2,256,256]{1,2,0:T(8,128)(2,1)} %fusion.29), channel_id=1, source_target_pairs={{4,0},{8,4},{12,8},{5,1},{9,5},{13,9},{6,2},{10,6},{14,10},{7,3},{... | collective-permute-start | bytes 786440 | tf_op jit(solution)/shard_map/ppermute | solution.py:19
  312.2 8.3 %copy-start.23 = (f32[256,64]{1,0:T(8,128)S(1)}, f32[256,64]{1,0:T(8,128)}, u32[]{:S(2)}) copy-start(f32[256,64]{1,0:T(8,128)} %copy-done.21) | copy-start | bytes 196612
  314.2 6.2 %copy-start.24 = (f32[256,4,64]{2,1,0:T(4,128)S(1)}, f32[256,4,64]{2,1,0:T(4,128)}, u32[]{:S(2)}) copy-start(f32[256,4,64]{2,1,0:T(4,128)} %copy.136) | copy-start | bytes 786436
  314.2 6.2 %copy-start.25 = (f32[256,4,64]{2,1,0:T(4,128)S(1)}, f32[256,4,64]{2,1,0:T(4,128)}, u32[]{:S(2)}) copy-start(f32[256,4,64]{2,1,0:T(4,128)} %copy.135) | copy-start | bytes 786436
  314.2 7.5 %copy-start.4 = (f32[256,4,128]{2,1,0:T(4,128)S(1)}, f32[256,4,128]{2,1,0:T(4,128)}, u32[]{:S(2)}) copy-start(f32[256,4,128]{2,1,0:T(4,128)} %copy-done.3) | copy-start | bytes 1572868
  319.1 13.9 %collective-permute-start.6 = (bf16[2,256,256]{1,2,0:T(8,128)(2,1)}, bf16[2,256,256]{1,2,0:T(8,128)(2,1)}, u32[]{:S(2)}, u32[]{:S(2)}) collective-permute-start(bf16[2,256,256]{1,2,0:T(8,128)(2,1)} %fusion.32), channel_id=1, source_target_pairs={{4,0},{8,4},{12,8},{5,1},{9,5},{13,9},{6,2},{10,6},{14,10},{7,3},{... | collective-permute-start | bytes 786440 | tf_op jit(solution)/shard_map/ppermute | solution.py:19
  320.8 15.4 %copy-start.28 = (f32[256,4]{1,0:T(8,128)S(1)}, f32[256,4]{1,0:T(8,128)}, u32[]{:S(2)}) copy-start(f32[256,4]{1,0:T(8,128)} %copy-done.27) | copy-start | bytes 12292
  334.7 13.9 %collective-permute-start.7 = (bf16[2,256,256]{1,2,0:T(8,128)(2,1)}, bf16[2,256,256]{1,2,0:T(8,128)(2,1)}, u32[]{:S(2)}, u32[]{:S(2)}) collective-permute-start(bf16[2,256,256]{1,2,0:T(8,128)(2,1)} %fusion.24), channel_id=1, source_target_pairs={{4,0},{8,4},{12,8},{5,1},{9,5},{13,9},{6,2},{10,6},{14,10},{7,3},{... | collective-permute-start | bytes 786440 | tf_op jit(solution)/shard_map/ppermute | solution.py:19
  338.2 11.4 %copy-start.9 = (bf16[256,4,128]{2,1,0:T(4,128)(2,1)}, bf16[256,4,128]{2,1,0:T(4,128)(2,1)S(1)}, u32[]{:S(2)}) copy-start(bf16[256,4,128]{2,1,0:T(4,128)(2,1)S(1)} %fusion.21) | copy-start | bytes 786436
  338.2 11.6 %copy-start.32 = (f32[256,64]{0,1:T(8,128)S(1)}, f32[256,64]{0,1:T(8,128)}, u32[]{:S(2)}) copy-start(f32[256,64]{0,1:T(8,128)} %copy.86) | copy-start | bytes 196612
  349.6 10.2 %copy-start.12 = (f32[2,256,256]{1,2,0:T(8,128)}, f32[2,256,256]{1,2,0:T(8,128)S(1)}, u32[]{:S(2)}) copy-start(f32[2,256,256]{1,2,0:T(8,128)S(1)} %fusion.33) | copy-start | bytes 1572868
  349.6 2.5 copy-start.30
  374.6 151.6 %reduce-scatter.9.cloned.1.call-start = ((), (), s32[]{:S(2)}) async-start(), calls=%async_computation.11 | async-start | bytes 3440640 | tf_op jit(solution)/shard_map/reduce_scatter | solution.py:202
  375.5 4.4 copy-start.5
  379.9 1.8 copy-start.11
  379.9 1.9 copy-start.13
  384.3 1.2 copy-start.26
  483.4 42.8 %copy-start.1 = (bf16[256,1344]{0,1:T(8,128)(2,1)S(1)}, bf16[256,1344]{0,1:T(8,128)(2,1)}, u32[]{:S(2)}) copy-start(bf16[256,1344]{0,1:T(8,128)(2,1)} %param.17) | copy-start | bytes 2064388
  (9 other events, 7.4 us)
Sparse Core Ops, SparseCore 0:
  9.6 59.6 all-gather.6
  70.9 25.0 all-gather.8
  97.5 26.3 all-gather.10
  125.3 45.5 all-gather.16
  172.3 45.6 all-gather.12
  220.8 27.1 reduce-scatter.6
  263.4 26.5 all-gather.14
  295.4 59.1 reduce-scatter.10
  374.7 94.5 reduce-scatter.12
  472.1 54.1 reduce-scatter.8
where the time goes:
time: 535 us; the launch traced here: 533 us
  waiting for transfers between devices  328 us (61%)
  local copies, waits for them, and re-layouts  63.6 us (12%)
  matrix products  63.2 us (12%)
  starting transfers between devices  38.1 us (7%)
  other arithmetic  25.4 us (5%)
  between operations  14.9 us (3%)
    unnamed x11, waiting for transfers between devices  77.9 us
    all_gather x1, waiting for transfers between devices, local(): full_rows = lax.all_gather(tokens, 'hid', axis=1, tiled=True)  57.2 us
    unnamed x90, local copies, waits for them, and re-layouts  41.8 us
    reduce_scatter x1, waiting for transfers between devices, local(): lax.psum_scatter(block_rows.astype(jnp.bfloat16), 'hid', scatter_dimensio...  38.4 us
    ppermute x8, starting transfers between devices, from_behind(): lax.ppermute(value, axis, [(source, source + steps) for source in range(f...  37 us
    all_gather x1, waiting for transfers between devices, local(): lax.all_gather(w_query, 'tok', axis=0, tiled=True)  29.4 us
    ppermute x8, waiting for transfers between devices, from_behind(): lax.ppermute(value, axis, [(source, source + steps) for source in range(f...  28.1 us
    all_gather x1, waiting for transfers between devices, local(): all_heads = lax.all_gather(attended, 'hid', axis=1, tiled=True)  26.7 us
  transfers between devices with their start and end apart: 18, of which 16 were waited for; matrix products, arithmetic and copies ran while one was open for 24% of the time, Pallas kernels for 0%

commit v1 on v0

--- a/solution.py
+++ b/solution.py
@@ -11,6 +11,12 @@
 attn_scale = 168.0 ** (-0.5)
 rope_base = 10000.0
 norm_eps = 1e-06
+
+
+def paths_remake(matrix, join_dim):
+    even = list(matrix.shape[1:])
+    even[join_dim] *= matrix.shape[0]
+    return jnp.moveaxis(matrix, 0, join_dim).reshape(even)
 
 
 def from_behind(value, axis, steps):
@@ -61,10 +67,34 @@
     query_cols = query_heads * HEAD_SIZE
     kv_cols = key_value_heads * HEAD_SIZE
     full_rows = lax.all_gather(tokens, "hid", axis=1, tiled=True)
+
+    def settle_array(local_values, axis_id, dim_at):
+        n_all = jax.lax.psum(1, axis_name=axis_id)
+        leaves = tuple(((s, (s + 1) % n_all) for s in range(n_all)))
+        arrivals = tuple(((j, p) for p, j in leaves))
+        w1, p_next = ([], [])
+        for j0 in range(n_all - 1):
+            if j0 % 2 == 0:
+                all_values = jax.lax.ppermute(
+                    w1[-1] if w1 else local_values, perm=leaves, axis_name=axis_id
+                )
+                w1.append(all_values)
+            else:
+                view_out = jax.lax.ppermute(
+                    p_next[-1] if p_next else local_values, axis_name=axis_id, perm=arrivals
+                )
+                p_next.append(view_out)
+        u_next = jnp.stack([*w1[::-1], local_values, *p_next])
+        x_next = jax.lax.axis_index(axis_id)
+        z = len(w1)
+        right_arr = x_next - z
+        u_next = u_next[(jnp.arange(n_all) - right_arr) % n_all]
+        return paths_remake(u_next, dim_at)
+
     pieces = (
         lax.all_gather(w_query, "tok", axis=0, tiled=True),
         lax.all_gather(key_weight, "tok", axis=0, tiled=True),
-        lax.all_gather(value_weight, "tok", axis=0, tiled=True),
+        settle_array(value_weight, "tok", 0),
     )
     columns = full_rows
     query_unnormed = jnp.dot(columns, pieces[0], preferred_element_type=jnp.float32)

time: 535 us -> 507 us (0.948)
  waiting for transfers between devices: 328 us -> 280 us
  starting transfers between devices: 38.1 us -> 47.5 us
  matrix products: 63.2 us -> 69.4 us
    all_gather x1, waiting for transfers between devices: 57.2 us -> 28.8 us  [local(): full_rows = lax.all_gather(tokens, 'hid', axis=1, tiled=True)]
    all_gather x1, waiting for transfers between devices: 20.9 us -> 0.01 us  [local(): lax.all_gather(value_weight, 'tok', axis=0, tiled=True)]
    ppermute x0 -> x3, waiting for transfers between devices: none -> 19.7 us  [the longest x2 19.7 us: settle_array(): jax.lax.ppermute(w1[-1] if w1 else local_values, perm=leaves, axis_name=a...]
    all_gather x1, waiting for transfers between devices: 29.4 us -> 18.4 us  [local(): lax.all_gather(w_query, 'tok', axis=0, tiled=True)]
    ppermute x8, waiting for transfers between devices: 28.1 us -> 21.8 us  [from_behind(): lax.ppermute(value, axis, [(source, source + steps) for source in range(f...]
    unnamed x90 -> x94, local copies, waits for them, and re-layouts: 41.8 us -> 40.8 us
  transfers between devices with their start and end apart: 18 -> 21, of which waited for: 16 -> 16; matrix products, arithmetic and copies ran while one was open for 24% -> 28% of each run, Pallas kernels for 0% -> 0%
where the time goes in v1:
time: 507 us; the launch traced here: 505 us
  waiting for transfers between devices  280 us (55%)
  matrix products  69.4 us (14%)
  local copies, waits for them, and re-layouts  64.8 us (13%)
  starting transfers between devices  47.5 us (9%)
  other arithmetic  28.4 us (6%)
  between operations  14.9 us (3%)
    unnamed x11, waiting for transfers between devices  78.1 us
    ppermute x8, starting transfers between devices, from_behind(): lax.ppermute(value, axis, [(source, source + steps) for source in range(f...  41.4 us
    unnamed x94, local copies, waits for them, and re-layouts  40.8 us
    reduce_scatter x1, waiting for transfers between devices, local(): lax.psum_scatter(block_rows.astype(jnp.bfloat16), 'hid', scatter_dimensio...  38.4 us
    all_gather x1, waiting for transfers between devices, local(): full_rows = lax.all_gather(tokens, 'hid', axis=1, tiled=True)  28.8 us
    all_gather x1, waiting for transfers between devices, local(): lax.all_gather(key_weight, 'tok', axis=0, tiled=True)  26.6 us
    all_gather x1, waiting for transfers between devices, local(): all_heads = lax.all_gather(attended, 'hid', axis=1, tiled=True)  25.9 us
    reduce_scatter x1, waiting for transfers between devices, local(): lax.psum_scatter(partial_heads.astype(jnp.bfloat16), 'hid', scatter_dimen...  22.1 us
  transfers between devices with their start and end apart: 21, of which 16 were waited for; matrix products, arithmetic and copies ran while one was open for 28% of the time, Pallas kernels for 0%

profile of v1, /device:TPU:0, one launch (start us, length us, event | category | flops | bytes accessed | tf_op | source)
XLA Modules:
  0.0 504.9 jit_solution(663102702426551453)
XLA Ops:
  10.6 2.0 collective-permute-start.2
  12.6 13.3 %collective-permute-done = bf16[1344,256]{1,0:T(8,128)(2,1)S(1)} collective-permute-done((bf16[1344,256]{1,0:T(8,128)(2,1)S(1)}, bf16[1344,256]{1,0:T(8,128)(2,1)S(1)}, u32[]{:S(2)}, u32[]{:S(2)}) %collective-permute-start) | collective-permute-done | bytes 688160 | tf_op jit(solution)/shard_map/ppermute | solution.py:78
  25.8 2.5 collective-permute-start.1
  29.9 6.5 %collective-permute-done.1 = bf16[1344,256]{1,0:T(8,128)(2,1)} collective-permute-done((bf16[1344,256]{1,0:T(8,128)(2,1)S(1)}, bf16[1344,256]{1,0:T(8,128)(2,1)}, u32[]{:S(2)}, u32[]{:S(2)}) %collective-permute-start.1) | collective-permute-done | bytes 688160 | tf_op jit(solution)/shard_map/ppermute | solution.py:78
  38.3 2.3 gather_fusion
  40.5 28.8 %all-gather.7.cloned.1.call-done = bf16[256,5376]{0,1:T(8,128)(2,1)} async-done(((bf16[256,1344]{0,1:T(8,128)(2,1)}), bf16[256,5376]{0,1:T(8,128)(2,1)}) %all-gather.7.cloned.1.call-update) | async-done | bytes 2752528 | tf_op jit(solution)/shard_map/all_gather | solution.py:69
  69.3 26.6 %all-gather.9.cloned.1.call-done = bf16[5376,256]{1,0:T(8,128)(2,1)} async-done(((bf16[1344,256]{1,0:T(8,128)(2,1)}), bf16[5376,256]{1,0:T(8,128)(2,1)}) %all-gather.9.cloned.1.call-update) | async-done | bytes 2752528 | tf_op jit(solution)/shard_map/all_gather | solution.py:96
  96.0 3.8 multiply_reduce_fusion.3
  103.0 3.3 fusion.17
  106.9 2.1 collective-permute-start.3
  110.9 10.4 %collective-permute-start.4 = (bf16[2,256,256]{2,1,0:T(8,128)(2,1)S(1)}, bf16[2,256,256]{2,1,0:T(8,128)(2,1)}, u32[]{:S(2)}, u32[]{:S(2)}) collective-permute-start(bf16[2,256,256]{2,1,0:T(8,128)(2,1)S(1)} %collective-permute-done.3), channel_id=1, source_target_pairs={{0,4},{4,8},{8,12},{1,5},{5,9},{9,13},{2,6},{6,10},{10,14},{3,7},{... | collective-permute-start | bytes 786440 | tf_op jit(solution)/shard_map/ppermute | solution.py:25
  121.8 12.7 %collective-permute-start.5 = (bf16[2,256,256]{2,1,0:T(8,128)(2,1)}, bf16[2,256,256]{2,1,0:T(8,128)(2,1)}, u32[]{:S(2)}, u32[]{:S(2)}) collective-permute-start(bf16[2,256,256]{2,1,0:T(8,128)(2,1)} %collective-permute-done.4), channel_id=1, source_target_pairs={{0,4},{4,8},{8,12},{1,5},{5,9},{9,13},{2,6},{6,10},{10,14},{3,7},{... | collective-permute-start | bytes 786440 | tf_op jit(solution)/shard_map/ppermute | solution.py:25
  135.3 10.9 %collective-permute-start.6 = (bf16[2,256,256]{2,1,0:T(8,128)(2,1)}, bf16[2,256,256]{2,1,0:T(8,128)(2,1)S(1)}, u32[]{:S(2)}, u32[]{:S(2)}) collective-permute-start(bf16[2,256,256]{2,1,0:T(8,128)(2,1)} %collective-permute-done.5), channel_id=1, source_target_pairs={{0,4},{4,8},{8,12},{1,5},{5,9},{9,13},{2,6},{6,10},{10,14},{3,7},{... | collective-permute-start | bytes 786440 | tf_op jit(solution)/shard_map/ppermute | solution.py:25
  146.2 2.1 fusion.11
  154.0 6.0 %convolution_convert_fusion.3 = bf16[256,2048]{1,0:T(8,128)(2,1)} fusion(bf16[256,1344]{0,1:T(8,128)(2,1)S(1)} %copy-done, bf16[2048,1344]{0,1:T(8,128)(2,1)} %all-gather.15.cloned.1.call-done), kind=kOutput, calls=%fused_computation.25 | convolution fusion | flops 1409810432 | bytes 7241728 | tf_op jit(solution)/shard_map/td,hd->th/dot_general | solution.py:155
  161.9 2.4 fusion.52
  164.4 2.5 reshape_squeeze.9
  166.9 2.5 reshape_squeeze.10
  169.4 2.9 copy.117
  172.3 18.4 %all-gather.11.cloned.1.call-done = bf16[5376,512]{1,0:T(8,128)(2,1)} async-done(((bf16[1344,512]{1,0:T(8,128)(2,1)}), bf16[5376,512]{1,0:T(8,128)(2,1)}) %all-gather.11.cloned.1.call-update) | async-done | bytes 5505040 | tf_op jit(solution)/shard_map/all_gather | solution.py:95
  190.8 5.0 fusion.55
  198.6 22.1 %reduce-scatter.7.cloned.1.call-done = bf16[256,512]{1,0:T(8,128)(2,1)} async-done(((bf16[256,2048]{1,0:T(8,128)(2,1)}), bf16[256,512]{1,0:T(8,128)(2,1)}) %reduce-scatter.7.cloned.1.call-update) | async-done | bytes 262160 | tf_op jit(solution)/shard_map/reduce_scatter | solution.py:161
  221.8 3.2 fusion.19
  225.0 7.2 %fusion.2 = (f32[2,2,256]{2,1,0:T(2,128)S(1)}, f32[2,2,256,1280]{2,3,1,0:T(8,128)}) fusion(f32[2,1280,256,2]{2,1,3,0:T(8,128)} %fusion.19, bf16[1280,2,128,1]{0,2,3,1:T(8,128)(2,1)S(1)} %copy-done.14, pred[256,1280]{0,1:T(8,128)(4,1)S(1)} %copy-done.36, bf16[256,2,2,64]{3,0,2,1:T(8,128)(2,1)S(1)} %bitcast.114, bf16[256,2,2,64]{3,0,2,1:T(8,128)(2,1)S(1)} %bitcast.116), kind=kOutput, calls=%fused_computation.9 | convolution fusion | flops 342623488 | bytes 11735040 | tf_op jit(solution)/shard_map/div | solution.py:141
  232.2 3.8 fusion.14
  236.8 25.9 %all-gather.13.cloned.1.call-done = bf16[256,2048]{0,1:T(8,128)(2,1)} async-done(((bf16[256,512]{0,1:T(8,128)(2,1)}), bf16[256,2048]{0,1:T(8,128)(2,1)}) %all-gather.13.cloned.1.call-update) | async-done | bytes 1048592 | tf_op jit(solution)/shard_map/all_gather | solution.py:147
  262.7 5.2 %convolution_convert_fusion.1 = bf16[2048,1344]{0,1:T(8,128)(2,1)} fusion(bf16[256,2048]{0,1:T(8,128)(2,1)} %all-gather.13.cloned.1.call-done, bf16[256,1344]{0,1:T(8,128)(2,1)S(1)} %copy-done), kind=kOutput, calls=%fused_computation.6 | convolution fusion | flops 1412038656 | bytes 7241728 | tf_op jit(solution)/shard_map/th,td->hd/dot_general | solution.py:167
  268.3 5.7 %fusion.4 = bf16[2,2,256,1280]{2,3,1,0:T(8,128)(2,1)S(1)} fusion(f32[2,1280,256,2]{2,1,3,0:T(8,128)} %fusion.19, f32[2,2,256,1280]{2,3,1,0:T(8,128)} %get-tuple-element.51, f32[2,2,256]{2,1,0:T(2,128)S(1)} %get-tuple-element.50), kind=kLoop, calls=%fused_computation.11 | loop fusion | flops 5242880 | bytes 13111296 | tf_op jit(solution)/shard_map/convert_element_type | solution.py:182
  275.1 3.5 fusion.7
  280.0 2.1 collective-permute-done.7
  286.8 8.9 %collective-permute-done.8 = bf16[2,256,256]{1,2,0:T(8,128)(2,1)} collective-permute-done((bf16[2,256,256]{1,2,0:T(8,128)(2,1)}, bf16[2,256,256]{1,2,0:T(8,128)(2,1)}, u32[]{:S(2)}, u32[]{:S(2)}) %collective-permute-start.8) | collective-permute-done | bytes 262176 | tf_op jit(solution)/shard_map/ppermute | solution.py:25
  300.7 5.0 collective-permute-done.9
  309.0 2.0 fusion.21
  311.8 3.4 collective-permute-done.10
  318.8 7.7 %fusion = bf16[5376,1024]{0,1:T(8,128)(2,1)} fusion(bf16[256,5376]{0,1:T(8,128)(2,1)} %all-gather.7.cloned.1.call-done, bf16[256,256]{1,0:T(8,128)(2,1)S(1)} %copy.109, bf16[256,256]{1,0:T(8,128)(2,1)S(1)} %copy.108, bf16[256,512]{1,0:T(8,128)(2,1)S(1)} %bitcast.113), kind=kOutput, calls=%fused_computation.2 | convolution fusion | flops 2825650176 | bytes 14286848 | tf_op jit(solution)/shard_map/td,tc->dc/dot_general | solution.py:238
  326.5 14.7 %copy.133 = bf16[5376,1024]{1,0:T(8,128)(2,1)} copy(bf16[5376,1024]{0,1:T(8,128)(2,1)} %fusion) | data formatting | bytes 22020096
  342.2 4.5 fusion.49
  346.7 3.3 convolution_add_fusion.1
  349.9 6.0 %fusion.1 = bf16[256,5376]{0,1:T(8,128)(2,1)} fusion(f32[256,5376]{0,1:T(8,128)} %convolution_add_fusion.1, bf16[5376,256]{1,0:T(8,128)(2,1)} %all-gather.17.cloned.1.call-done, f32[2,256,256]{1,2,0:T(8,128)S(1)} %copy-done.13), kind=kOutput, calls=%fused_computation.5 | convolution fusion | flops 707395584 | bytes 11141120 | tf_op jit(solution)/shard_map/tc,dc->td/dot_general | solution.py:229
  357.1 5.6 %convolution_convert_fusion.2 = bf16[256,1344]{0,1:T(8,128)(2,1)} fusion(bf16[2048,1344]{0,1:T(8,128)(2,1)} %all-gather.15.cloned.1.call-done, bf16[256,2048]{0,1:T(8,128)(2,1)S(1)} %copy-done.26), kind=kOutput, calls=%fused_computation.24 | convolution fusion | flops 1409630208 | bytes 7241728 | tf_op jit(solution)/shard_map/dot_general | solution.py:149
  362.7 3.7 convert_element_type.115
  366.4 74.7 %reduce-scatter.13.cloned.1.call-done = bf16[1344,1024]{1,0:T(8,128)(2,1)} async-done(((bf16[5376,1024]{1,0:T(8,128)(2,1)}), bf16[1344,1024]{1,0:T(8,128)(2,1)}) %reduce-scatter.13.cloned.1.call-update) | async-done | bytes 2752528
  441.1 4.5 copy.134
  445.6 3.2 slice.84
  448.8 3.8 copy.110
  452.6 2.6 fusion.51
  455.2 2.9 copy.111
  459.6 38.4 %reduce-scatter.9.cloned.1.call-done = bf16[256,1344]{0,1:T(8,128)(2,1)} async-done(((bf16[256,5376]{0,1:T(8,128)(2,1)}), bf16[256,1344]{0,1:T(8,128)(2,1)}) %reduce-scatter.9.cloned.1.call-update) | async-done | bytes 688144 | tf_op jit(solution)/shard_map/reduce_scatter | solution.py:232
  (171 shorter events, 49.5 us)
Async XLA Ops:
  7.2 146.9 %copy-start = (bf16[256,1344]{0,1:T(8,128)(2,1)S(1)}, bf16[256,1344]{0,1:T(8,128)(2,1)}, u32[]{:S(2)}) copy-start(bf16[256,1344]{0,1:T(8,128)(2,1)} %param.17) | copy-start | bytes 2064388
  7.2 21.2 %copy-start.38 = (s32[1024]{0:T(1024)S(1)}, s32[1024]{0:T(1024)}, u32[]{:S(2)}) copy-start(s32[1024]{0:T(1024)} %param.16) | copy-start | bytes 12292
  7.2 62.1 %all-gather.7.cloned.1.call-start = ((), (), s32[]{:S(2)}) async-start(), calls=%async_computation.4 | async-start | bytes 3440640 | tf_op jit(solution)/shard_map/all_gather | solution.py:69
  7.9 88.0 %all-gather.9.cloned.1.call-start = ((), (), s32[]{:S(2)}) async-start(), calls=%async_computation.5 | async-start | bytes 3440640 | tf_op jit(solution)/shard_map/all_gather | solution.py:96
  8.7 145.3 %all-gather.15.cloned.1.call-start = ((), (), s32[]{:S(2)}) async-start(), calls=%async_computation.8 | async-start | bytes 6881280 | tf_op jit(solution)/shard_map/all_gather | solution.py:151
  9.4 181.3 %all-gather.11.cloned.1.call-start = ((), (), s32[]{:S(2)}) async-start(), calls=%async_computation.6 | async-start | bytes 6881280 | tf_op jit(solution)/shard_map/all_gather | solution.py:95
  10.0 210.7 %reduce-scatter.7.cloned.1.call-start = ((), (), s32[]{:S(2)}) async-start(), calls=%async_computation.9 | async-start | bytes 1310720 | tf_op jit(solution)/shard_map/reduce_scatter | solution.py:161
  10.1 15.8 %collective-permute-start = (bf16[1344,256]{1,0:T(8,128)(2,1)S(1)}, bf16[1344,256]{1,0:T(8,128)(2,1)S(1)}, u32[]{:S(2)}, u32[]{:S(2)}) collective-permute-start(bf16[1344,256]{1,0:T(8,128)(2,1)S(1)} %copy-done.11), channel_id=1, source_target_pairs={{0,4},{4,8},{8,12},{12,0},{1,5},{5,9},{9,13},{13,1},{2,6},{6,10},{... | collective-permute-start | bytes 2064392 | tf_op jit(solution)/shard_map/ppermute | solution.py:78
  10.6 19.3 %collective-permute-start.2 = (bf16[1344,256]{1,0:T(8,128)(2,1)S(1)}, bf16[1344,256]{1,0:T(8,128)(2,1)S(1)}, u32[]{:S(2)}, u32[]{:S(2)}) collective-permute-start(bf16[1344,256]{1,0:T(8,128)(2,1)S(1)} %copy-done.11), channel_id=1, source_target_pairs={{4,0},{8,4},{12,8},{0,12},{5,1},{9,5},{13,9},{1,13},{6,2},{10,6},{... | collective-permute-start | bytes 2064392 | tf_op jit(solution)/shard_map/ppermute | solution.py:83
  25.8 10.5 %copy-start.31 = (bf16[1344,256]{1,0:T(8,128)(2,1)}, bf16[1344,256]{1,0:T(8,128)(2,1)S(1)}, u32[]{:S(2)}) copy-start(bf16[1344,256]{1,0:T(8,128)(2,1)S(1)} %collective-permute-done) | copy-start | bytes 2064388
  25.8 10.5 %collective-permute-start.1 = (bf16[1344,256]{1,0:T(8,128)(2,1)S(1)}, bf16[1344,256]{1,0:T(8,128)(2,1)}, u32[]{:S(2)}, u32[]{:S(2)}) collective-permute-start(bf16[1344,256]{1,0:T(8,128)(2,1)S(1)} %collective-permute-done), channel_id=1, source_target_pairs={{0,4},{4,8},{8,12},{12,0},{1,5},{5,9},{9,13},{13,1},{2,6},{6,10},{... | collective-permute-start | bytes 2064392 | tf_op jit(solution)/shard_map/ppermute | solution.py:78
  29.0 7.3 %copy-start.19 = (f32[256,64]{1,0:T(8,128)}, f32[256,64]{1,0:T(8,128)S(1)}, u32[]{:S(2)}) copy-start(f32[256,64]{1,0:T(8,128)S(1)} %get-tuple-element.46) | copy-start | bytes 196612
  29.0 7.3 %copy-start.21 = (f32[256,64]{1,0:T(8,128)}, f32[256,64]{1,0:T(8,128)S(1)}, u32[]{:S(2)}) copy-start(f32[256,64]{1,0:T(8,128)S(1)} %get-tuple-element.47) | copy-start | bytes 196612
  29.8 6.5 %copy-start.32 = (bf16[1344,256]{1,0:T(8,128)(2,1)}, bf16[1344,256]{1,0:T(8,128)(2,1)S(1)}, u32[]{:S(2)}) copy-start(bf16[1344,256]{1,0:T(8,128)(2,1)S(1)} %collective-permute-done.2) | copy-start | bytes 2064388
  40.5 60.0 %copy-start.40 = (f32[128]{0:T(128)S(1)}, f32[128]{0:T(128)}, u32[]{:S(2)}) copy-start(f32[128]{0:T(128)} %param.15) | copy-start | bytes 1540
  69.3 33.6 %copy-start.2 = (bf16[256,5376]{0,1:T(8,128)(2,1)S(1)}, bf16[256,5376]{0,1:T(8,128)(2,1)}, u32[]{:S(2)}) copy-start(bf16[256,5376]{0,1:T(8,128)(2,1)} %all-gather.7.cloned.1.call-done) | copy-start | bytes 8257540
  96.0 4.6 copy-start.33
  103.0 3.3 copy-start.29
  106.9 3.3 collective-permute-start.3
  110.9 10.9 %collective-permute-start.4 = (bf16[2,256,256]{2,1,0:T(8,128)(2,1)S(1)}, bf16[2,256,256]{2,1,0:T(8,128)(2,1)}, u32[]{:S(2)}, u32[]{:S(2)}) collective-permute-start(bf16[2,256,256]{2,1,0:T(8,128)(2,1)S(1)} %collective-permute-done.3), channel_id=1, source_target_pairs={{0,4},{4,8},{8,12},{1,5},{5,9},{9,13},{2,6},{6,10},{10,14},{3,7},{... | collective-permute-start | bytes 786440 | tf_op jit(solution)/shard_map/ppermute | solution.py:25
  121.8 13.5 %collective-permute-start.5 = (bf16[2,256,256]{2,1,0:T(8,128)(2,1)}, bf16[2,256,256]{2,1,0:T(8,128)(2,1)}, u32[]{:S(2)}, u32[]{:S(2)}) collective-permute-start(bf16[2,256,256]{2,1,0:T(8,128)(2,1)} %collective-permute-done.4), channel_id=1, source_target_pairs={{0,4},{4,8},{8,12},{1,5},{5,9},{9,13},{2,6},{6,10},{10,14},{3,7},{... | collective-permute-start | bytes 786440 | tf_op jit(solution)/shard_map/ppermute | solution.py:25
  135.3 13.0 %collective-permute-start.6 = (bf16[2,256,256]{2,1,0:T(8,128)(2,1)}, bf16[2,256,256]{2,1,0:T(8,128)(2,1)S(1)}, u32[]{:S(2)}, u32[]{:S(2)}) collective-permute-start(bf16[2,256,256]{2,1,0:T(8,128)(2,1)} %collective-permute-done.5), channel_id=1, source_target_pairs={{0,4},{4,8},{8,12},{1,5},{5,9},{9,13},{2,6},{6,10},{10,14},{3,7},{... | collective-permute-start | bytes 786440 | tf_op jit(solution)/shard_map/ppermute | solution.py:25
  160.0 102.7 %all-gather.13.cloned.1.call-start = ((), (), s32[]{:S(2)}) async-start(), calls=%async_computation.7 | async-start | bytes 1310720 | tf_op jit(solution)/shard_map/all_gather | solution.py:147
  172.3 25.3 %copy-start.39 = (f32[128]{0:T(128)S(1)}, f32[128]{0:T(128)}, u32[]{:S(2)}) copy-start(f32[128]{0:T(128)} %param.14) | copy-start | bytes 1540
  197.0 24.8 %copy-start.3 = (f32[256,4,128]{2,1,0:T(4,128)}, f32[256,4,128]{2,1,0:T(4,128)S(1)}, u32[]{:S(2)}) copy-start(f32[256,4,128]{2,1,0:T(4,128)S(1)} %reshape.277) | copy-start | bytes 1572868
  197.0 24.8 %copy-start.6 = (bf16[1280,2,128]{2,1,0:T(2,128)(2,1)S(1)}, bf16[1280,2,128]{2,1,0:T(2,128)(2,1)}, u32[]{:S(2)}) copy-start(bf16[1280,2,128]{2,1,0:T(2,128)(2,1)} %reshape_squeeze.9) | copy-start | bytes 1966084
  197.6 24.2 %copy-start.27 = (f32[256,4]{1,0:T(8,128)}, f32[256,4]{1,0:T(8,128)S(1)}, u32[]{:S(2)}) copy-start(f32[256,4]{1,0:T(8,128)S(1)} %copy.90) | copy-start | bytes 12292
  221.8 3.2 copy-start.17
  236.0 113.9 %all-gather.17.cloned.1.call-start = ((), (), s32[]{:S(2)}) async-start(), calls=%async_computation.10 | async-start | bytes 3440640 | tf_op jit(solution)/shard_map/all_gather | solution.py:223
  236.7 126.0 %reduce-scatter.11.cloned.1.call-start = ((), (), s32[]{:S(2)}) async-start(), calls=%async_computation.12 | async-start | bytes 6881280 | tf_op jit(solution)/shard_map/reduce_scatter | solution.py:166
  268.0 173.1 %reduce-scatter.13.cloned.1.call-start = ((), (), s32[]{:S(2)}) async-start(), calls=%async_computation.13 | async-start | bytes 13762560
  278.6 5.7 %copy-start.15 = (bf16[1280,2,128,1]{0,2,3,1:T(8,128)(2,1)S(1)}, bf16[1280,2,128,1]{0,2,3,1:T(8,128)(2,1)}, u32[]{:S(2)}) copy-start(bf16[1280,2,128,1]{0,2,3,1:T(8,128)(2,1)} %copy.117) | copy-start | bytes 1966084
  278.6 3.6 collective-permute-start.7
  282.9 12.8 %collective-permute-start.8 = (bf16[2,256,256]{1,2,0:T(8,128)(2,1)}, bf16[2,256,256]{1,2,0:T(8,128)(2,1)}, u32[]{:S(2)}, u32[]{:S(2)}) collective-permute-start(bf16[2,256,256]{1,2,0:T(8,128)(2,1)} %fusion.29), channel_id=1, source_target_pairs={{4,0},{8,4},{12,8},{5,1},{9,5},{13,9},{6,2},{10,6},{14,10},{7,3},{... | collective-permute-start | bytes 786440 | tf_op jit(solution)/shard_map/ppermute | solution.py:25
  284.8 13.9 %copy-start.23 = (f32[256,64]{1,0:T(8,128)S(1)}, f32[256,64]{1,0:T(8,128)}, u32[]{:S(2)}) copy-start(f32[256,64]{1,0:T(8,128)} %copy-done.21) | copy-start | bytes 196612
  286.8 11.9 %copy-start.24 = (f32[256,4,64]{2,1,0:T(4,128)S(1)}, f32[256,4,64]{2,1,0:T(4,128)}, u32[]{:S(2)}) copy-start(f32[256,4,64]{2,1,0:T(4,128)} %copy.136) | copy-start | bytes 786436
  286.8 11.9 %copy-start.25 = (f32[256,4,64]{2,1,0:T(4,128)S(1)}, f32[256,4,64]{2,1,0:T(4,128)}, u32[]{:S(2)}) copy-start(f32[256,4,64]{2,1,0:T(4,128)} %copy.135) | copy-start | bytes 786436
  286.8 13.2 %copy-start.4 = (f32[256,4,128]{2,1,0:T(4,128)S(1)}, f32[256,4,128]{2,1,0:T(4,128)}, u32[]{:S(2)}) copy-start(f32[256,4,128]{2,1,0:T(4,128)} %copy-done.3) | copy-start | bytes 1572868
  297.4 8.4 %collective-permute-start.9 = (bf16[2,256,256]{1,2,0:T(8,128)(2,1)}, bf16[2,256,256]{1,2,0:T(8,128)(2,1)}, u32[]{:S(2)}, u32[]{:S(2)}) collective-permute-start(bf16[2,256,256]{1,2,0:T(8,128)(2,1)} %fusion.32), channel_id=1, source_target_pairs={{4,0},{8,4},{12,8},{5,1},{9,5},{13,9},{6,2},{10,6},{14,10},{7,3},{... | collective-permute-start | bytes 786440 | tf_op jit(solution)/shard_map/ppermute | solution.py:25
  299.1 9.9 %copy-start.28 = (f32[256,4]{1,0:T(8,128)S(1)}, f32[256,4]{1,0:T(8,128)}, u32[]{:S(2)}) copy-start(f32[256,4]{1,0:T(8,128)} %copy-done.27) | copy-start | bytes 12292
  307.5 7.6 %collective-permute-start.10 = (bf16[2,256,256]{1,2,0:T(8,128)(2,1)}, bf16[2,256,256]{1,2,0:T(8,128)(2,1)}, u32[]{:S(2)}, u32[]{:S(2)}) collective-permute-start(bf16[2,256,256]{1,2,0:T(8,128)(2,1)} %fusion.24), channel_id=1, source_target_pairs={{4,0},{8,4},{12,8},{5,1},{9,5},{13,9},{6,2},{10,6},{14,10},{7,3},{... | collective-permute-start | bytes 786440 | tf_op jit(solution)/shard_map/ppermute | solution.py:25
  311.0 5.2 %copy-start.9 = (bf16[256,4,128]{2,1,0:T(4,128)(2,1)}, bf16[256,4,128]{2,1,0:T(4,128)(2,1)S(1)}, u32[]{:S(2)}) copy-start(bf16[256,4,128]{2,1,0:T(4,128)(2,1)S(1)} %fusion.21) | copy-start | bytes 786436
  311.0 5.4 %copy-start.34 = (f32[256,64]{0,1:T(8,128)S(1)}, f32[256,64]{0,1:T(8,128)}, u32[]{:S(2)}) copy-start(f32[256,64]{0,1:T(8,128)} %copy.86) | copy-start | bytes 196612
  316.2 10.3 %copy-start.12 = (f32[2,256,256]{1,2,0:T(8,128)}, f32[2,256,256]{1,2,0:T(8,128)S(1)}, u32[]{:S(2)}) copy-start(f32[2,256,256]{1,2,0:T(8,128)S(1)} %fusion.33) | copy-start | bytes 1572868
  341.3 156.8 %reduce-scatter.9.cloned.1.call-start = ((), (), s32[]{:S(2)}) async-start(), calls=%async_computation.11 | async-start | bytes 3440640 | tf_op jit(solution)/shard_map/reduce_scatter | solution.py:232
  342.2 4.5 copy-start.5
  346.7 3.3 copy-start.13
  455.2 42.8 %copy-start.1 = (bf16[256,1344]{0,1:T(8,128)(2,1)S(1)}, bf16[256,1344]{0,1:T(8,128)(2,1)}, u32[]{:S(2)}) copy-start(bf16[256,1344]{0,1:T(8,128)(2,1)} %param.17) | copy-start | bytes 2064388
  (14 other events, 23.4 us)
Sparse Core Ops, SparseCore 0:
  9.6 59.6 all-gather.6
  70.9 25.0 all-gather.8
  97.5 46.0 all-gather.14
  145.0 45.7 all-gather.10
  193.5 27.1 reduce-scatter.6
  236.1 26.5 all-gather.12
  264.4 28.5 all-gather.16
  295.7 55.3 reduce-scatter.10
  353.6 87.4 reduce-scatter.12
  443.8 54.1 reduce-scatter.8
